TPU v7x, 32 devices: a whole 2x2x4 slice. The times are simulated.
32 devices in a mesh: gx: 4 (over x, core), gy: 2 (over y), sa: 4 (over z).
Axes of the slice: x: 2, y: 2, z: 4, core: 2. Of those that a mesh axis runs over, the one named last changes fastest.
Arguments:
- green: bfloat16 [8, 4, 2, 2, 1024, 256], P('gx', 'gy', None, None, 'sa'), may hold values from -0.59765625 to 0.59765625
- offsets: int32 [4, 2], replicated, may hold values from -1 to 1, as said below
Outputs:
- hessian: float32 [8, 4, 4, 2, 256, 512], P('gx', 'gy', None, None, 'sa')
Inputs may be any that keep to these rules, and one draw needn't show every extreme that they name: `offsets`: each row is an offset (dx, dy) within 1 tiles with dx >= 0, and dy >= 0 where dx = 0; rows are distinct; (1, -1) and (1, 1) are always among them.
All inputs are finite; a program needn't handle non-finite values.
Results may differ from a plain program's by a relative error of at most 0.0003.
Values may be sent and summed in bfloat16 or wider, within the bound.
A program may use at most 128 MiB of HBM per device.

v0:
```python
import jax
import jax.numpy as jnp
from jax import lax
from jax.sharding import PartitionSpec as P

NPAIR = 4


def from_behind(value, axis, steps):
    count = lax.axis_size(axis)
    initial, last = (max(0, -steps), min(count, count - steps))
    return lax.ppermute(value, axis, [(source, source + steps) for source in range(initial, last)])


def with_halo(shard, sides, width):
    for axis, dim in sides:
        size, length = (lax.axis_size(axis), shard.shape[dim])
        up = [(i, (i + 1) % size) for i in range(size - 1)]
        down = [(j, i) for i, j in up]
        last = lax.slice_in_dim(shard, length - width, length, axis=dim)
        initial = lax.slice_in_dim(shard, 0, width, axis=dim)
        before = lax.ppermute(last, axis, up)
        after = lax.ppermute(initial, axis, down)
        shard = jnp.concatenate([before, shard, after], axis=dim)
    return shard


def per_device(green, offsets):
    tiles_x = green.shape[0]
    tiles_y = green.shape[1]
    frequencies = green.shape[2]
    traces = green.shape[4]
    points = green.shape[5]
    following = from_behind(green[:1], "gx", -1)
    longer = jnp.concatenate([green, following], axis=0)
    widened = with_halo(longer, (("gy", 1),), 1)
    count = tiles_x * tiles_y * frequencies
    left = green.reshape(count, 2 * traces, points)
    zero = jnp.int32(0)

    def pair_term(index):
        start_x = offsets[index, 0]
        start_y = 1 + offsets[index, 1]
        beside = lax.dynamic_slice(widened, (start_x, start_y, zero, zero, zero, zero), green.shape)
        real_rows = beside.reshape(count, 2 * traces, points)
        imag_rows = jnp.concatenate([beside[:, :, :, 1], -beside[:, :, :, 0]], axis=3).reshape(
            count, 2 * traces, points
        )
        right = jnp.concatenate([real_rows, imag_rows], axis=2)
        block = jnp.einsum("nsp,nsq->npq", left, right, preferred_element_type=jnp.float32)
        return block.reshape(tiles_x, tiles_y, frequencies, points, 2 * points)

    terms = jnp.stack([pair_term(index) for index in range(NPAIR)], axis=2)
    return lax.psum_scatter(terms, "sa", scatter_dimension=4, tiled=True)


def solution(mesh):
    return jax.shard_map(
        per_device,
        mesh=mesh,
        in_specs=(P("gx", "gy", None, None, "sa", None), P()),
        out_specs=P("gx", "gy", None, None, "sa", None),
        check_vma=False,
    )
```

profile of v0, /device:TPU:4, one launch (start us, length us, event | category | flops | bytes accessed | tf_op | source)
XLA Modules:
  0.0 441.4 jit_solution(14763115799212059349)
XLA Ops:
  15.6 6.8 %collective-permute-start.2 = (bf16[3,1,2,2,256,256]{5,4,3,2,1,0:T(8,128)(2,1)}, bf16[3,1,2,2,256,256]{5,4,3,2,1,0:T(8,128)(2,1)}, u32[]{:S(2)}, u32[]{:S(2)}) collective-permute-start(bf16[3,1,2,2,256,256]{5,4,3,2,1,0:T(8,128)(2,1)} %get-tuple-element.18), channel_id=1, source_target_pairs={{4,0},{5,1},{6,2},{7,3},{12,8},{13,9},{14,10},{15,11},{20,16},{21,... | collective-permute-start | bytes 4718600 | tf_op jit(solution)/shard_map/ppermute | solution.py:23
  35.7 7.2 %collective-permute-done.1 = bf16[3,1,2,2,256,256]{5,4,3,2,1,0:T(8,128)(2,1)} collective-permute-done((bf16[3,1,2,2,256,256]{5,4,3,2,1,0:T(8,128)(2,1)}, bf16[3,1,2,2,256,256]{5,4,3,2,1,0:T(8,128)(2,1)}, u32[]{:S(2)}, u32[]{:S(2)}) %collective-permute-start.1) | collective-permute-done | bytes 1572896 | tf_op jit(solution)/shard_map/ppermute | solution.py:22
  42.9 2.9 collective-permute-done.2
  45.8 2.9 pad_maximum_fusion.1
  48.7 2.9 constant_dynamic-slice_fusion.7
  51.6 3.1 constant_dynamic-slice_fusion.3
  54.7 2.3 copy.4
  61.5 2.3 copy.11
  63.8 2.3 copy.10
  68.3 2.3 copy.7
  71.9 4.0 copy.19
  75.9 5.8 %fusion = f32[8,512,256]{2,1,0:T(8,128)} fusion(bf16[8,512,256]{2,1,0:T(8,128)(2,1)} %bitcast.45, bf16[8,256,256]{1,2,0:T(8,128)(2,1)} %bitcast.60, bf16[8,256,256]{1,2,0:T(8,128)(2,1)S(1)} %bitcast.59, bf16[8,512,256]{1,2,0:T(8,128)(2,1)} %copy.19), kind=kOutput, calls=%fused_computation.2 | convolution fusion | flops 1086324736 | bytes 10485760 | tf_op jit(solution)/shard_map/nsp,nsq->npq/dot_general | solution.py:50
  81.8 5.3 %copy.15 = f32[2,2,1,2,256,512]{5,4,3,2,1,0:T(8,128)} copy(f32[2,2,1,2,256,512]{4,5,3,1,0,2:T(8,128)} %bitcast.49) | data formatting | bytes 8388608 | tf_op jit(solution)/shard_map/stack;reshape | solution.py:53
  87.0 4.0 copy.22
  91.0 5.8 %fusion.18 = f32[8,512,256]{2,1,0:T(8,128)} fusion(bf16[8,512,256]{2,1,0:T(8,128)(2,1)} %bitcast.46, bf16[8,256,256]{1,2,0:T(8,128)(2,1)S(1)} %bitcast.57, bf16[8,256,256]{1,2,0:T(8,128)(2,1)} %bitcast.58, bf16[8,512,256]{1,2,0:T(8,128)(2,1)} %copy.22), kind=kOutput, calls=%fused_computation.20 | convolution fusion | flops 1086324736 | bytes 10485760 | tf_op jit(solution)/shard_map/nsp,nsq->npq/dot_general | solution.py:50
  96.8 5.3 %copy.18 = f32[2,2,1,2,256,512]{5,4,3,2,1,0:T(8,128)} copy(f32[2,2,1,2,256,512]{4,5,3,1,0,2:T(8,128)} %bitcast.50) | data formatting | bytes 8388608 | tf_op jit(solution)/shard_map/stack;reshape | solution.py:53
  102.1 4.0 copy.21
  106.1 5.8 %fusion.12 = f32[8,512,256]{2,1,0:T(8,128)} fusion(bf16[8,512,256]{2,1,0:T(8,128)(2,1)} %bitcast.47, bf16[8,256,256]{1,2,0:T(8,128)(2,1)S(1)} %bitcast.55, bf16[8,256,256]{1,2,0:T(8,128)(2,1)} %bitcast.56, bf16[8,512,256]{1,2,0:T(8,128)(2,1)} %copy.21), kind=kOutput, calls=%fused_computation.14 | convolution fusion | flops 1086324736 | bytes 10485760 | tf_op jit(solution)/shard_map/nsp,nsq->npq/dot_general | solution.py:50
  111.9 5.3 %copy.17 = f32[2,2,1,2,256,512]{5,4,3,2,1,0:T(8,128)} copy(f32[2,2,1,2,256,512]{4,5,3,1,0,2:T(8,128)} %bitcast.51) | data formatting | bytes 8388608 | tf_op jit(solution)/shard_map/stack;reshape | solution.py:53
  117.2 2.4 copy.20
  119.6 5.8 %fusion.6 = f32[8,512,256]{2,1,0:T(8,128)} fusion(bf16[8,512,256]{2,1,0:T(8,128)(2,1)} %bitcast.48, bf16[8,256,256]{1,2,0:T(8,128)(2,1)S(1)} %bitcast.53, bf16[8,256,256]{1,2,0:T(8,128)(2,1)} %bitcast.54, bf16[8,512,256]{1,2,0:T(8,128)(2,1)} %copy.20), kind=kOutput, calls=%fused_computation.8 | convolution fusion | flops 1086324736 | bytes 10485760 | tf_op jit(solution)/shard_map/nsp,nsq->npq/dot_general | solution.py:50
  125.4 5.3 %copy.16 = f32[2,2,1,2,256,512]{5,4,3,2,1,0:T(8,128)} copy(f32[2,2,1,2,256,512]{4,5,3,1,0,2:T(8,128)} %bitcast.52) | data formatting | bytes 8388608 | tf_op jit(solution)/shard_map/stack;reshape | solution.py:53
  130.7 11.6 %pad_maximum_fusion = f32[2,2,4,2,256,512]{5,4,3,2,1,0:T(8,128)} fusion(f32[2,2,1,2,256,512]{5,4,3,2,1,0:T(8,128)} %copy.18, f32[2,2,1,2,256,512]{5,4,3,2,1,0:T(8,128)} %copy.17, f32[2,2,1,2,256,512]{5,4,3,2,1,0:T(8,128)} %copy.16, f32[2,2,1,2,256,512]{5,4,3,2,1,0:T(8,128)} %copy.15), kind=kLoop, calls=%fused_computation | loop fusion | flops 12582912 | bytes 33554432 | tf_op jit(solution)/shard_map/stack | solution.py:53
  142.3 292.2 %reduce-scatter.2.cloned.1.call-done = f32[2,2,4,2,64,512]{5,4,3,2,1,0:T(8,128)} async-done(((f32[2,2,4,2,256,512]{5,4,3,2,1,0:T(8,128)}), f32[2,2,4,2,64,512]{5,4,3,2,1,0:T(8,128)}) %reduce-scatter.2.cloned.1.call-update) | async-done | bytes 4194320 | tf_op jit(solution)/shard_map/reduce_scatter | solution.py:54
  (24 shorter events, 17.8 us)
Async XLA Ops:
  6.5 428.1 %reduce-scatter.2.cloned.1.call-start = ((), (), s32[]{:S(2)}) async-start(), calls=%async_computation.1 | async-start | bytes 20971520 | tf_op jit(solution)/shard_map/reduce_scatter | solution.py:54
  7.8 4.6 %collective-permute-start = (bf16[1,2,2,2,256,256]{5,4,3,2,1,0:T(8,128)(2,1)S(1)}, bf16[1,2,2,2,256,256]{5,4,3,2,1,0:T(8,128)(2,1)S(1)}, u32[]{:S(2)}, u32[]{:S(2)}) collective-permute-start(bf16[1,2,2,2,256,256]{5,4,3,2,1,0:T(8,128)(2,1)S(1)} %slice.57), channel_id=1, source_target_pairs={{8,0},{16,8},{24,16},{9,1},{17,9},{25,17},{10,2},{18,10},{26,18},{... | collective-permute-start | bytes 3145736 | tf_op jit(solution)/shard_map/ppermute | solution.py:12
  10.9 11.6 %copy-start.4 = (s32[4,2]{0,1:T(2,128)S(1)}, s32[4,2]{0,1:T(2,128)}, u32[]{:S(2)}) copy-start(s32[4,2]{0,1:T(2,128)} %param.3) | copy-start | bytes 100
  14.4 28.5 %collective-permute-start.1 = (bf16[3,1,2,2,256,256]{5,4,3,2,1,0:T(8,128)(2,1)}, bf16[3,1,2,2,256,256]{5,4,3,2,1,0:T(8,128)(2,1)}, u32[]{:S(2)}, u32[]{:S(2)}) collective-permute-start(bf16[3,1,2,2,256,256]{5,4,3,2,1,0:T(8,128)(2,1)} %get-tuple-element.17), channel_id=1, source_target_pairs={{0,4},{1,5},{2,6},{3,7},{8,12},{9,13},{10,14},{11,15},{16,20},{17,... | collective-permute-start | bytes 4718600 | tf_op jit(solution)/shard_map/ppermute | solution.py:22
  15.6 30.1 %collective-permute-start.2 = (bf16[3,1,2,2,256,256]{5,4,3,2,1,0:T(8,128)(2,1)}, bf16[3,1,2,2,256,256]{5,4,3,2,1,0:T(8,128)(2,1)}, u32[]{:S(2)}, u32[]{:S(2)}) collective-permute-start(bf16[3,1,2,2,256,256]{5,4,3,2,1,0:T(8,128)(2,1)} %get-tuple-element.18), channel_id=1, source_target_pairs={{4,0},{5,1},{6,2},{7,3},{12,8},{13,9},{14,10},{15,11},{20,16},{21,... | collective-permute-start | bytes 4718600 | tf_op jit(solution)/shard_map/ppermute | solution.py:23
  71.9 4.0 copy-start.3
  87.0 4.0 copy-start.2
  102.1 4.0 copy-start.1
  117.2 2.4 copy-start
Sparse Core Ops, SparseCore 0:
  142.5 292.0 reduce-scatter.1
where the time goes:
time: 444 us; the launch traced here: 441 us
  waiting for transfers between devices  304 us (68%)
  local copies, waits for them, and re-layouts  61.3 us (14%)
  between operations  25.9 us (6%)
  matrix products  23.3 us (5%)
  other arithmetic  17.7 us (4%)
  starting transfers between devices  9.41 us (2%)
    reduce_scatter x1, waiting for transfers between devices, per_device(): return lax.psum_scatter(terms, 'sa', scatter_dimension=4, tiled=True)  292 us
    dot_general x4, matrix products, pair_term(): jnp.einsum('nsp,nsq->npq', left, right, preferred_element_type=jnp.float32)  23.3 us
    another operation x4, local copies, waits for them, and re-layouts, per_device(): terms = jnp.stack([pair_term(index) for index in range(NPAIR)], axis=2)  21 us
    reshape x4, local copies, waits for them, and re-layouts, pair_term(): real_rows = beside.reshape(count, 2 * traces, points)  14.4 us
    another operation x1, other arithmetic, per_device(): terms = jnp.stack([pair_term(index) for index in range(NPAIR)], axis=2)  11.6 us
    slice x4, local copies, waits for them, and re-layouts, pair_term(): beside[:, :, :, 1]  9.15 us
  transfers between devices with their start and end apart: 4, of which 4 were waited for; matrix products, arithmetic and copies ran while one was open for 1% of the time, Pallas kernels for 0%

commit v1 on v0

v1 whole, which is shorter than its diff:
```python
import functools

import jax
import jax.numpy as jnp
from jax import lax
from jax.experimental import pallas as pl
from jax.experimental.pallas import tpu as pltpu
from jax.sharding import PartitionSpec as P

MESH = pl.DeviceIdType.MESH
CANDIDATES = ((0, 0), (0, 1), (1, -1), (1, 0), (1, 1))


def kernel(
    nx, ny, nz, green, out, own, up, down, right, turned, left,
    load_sem, own_sem, up_sem, down_sem, right_sem,
    send_zu, send_zd, send_yu, send_yd, send_x,
):
    tiles_x, tiles_y, freqs, _, _, traces, points = own.shape
    width = points // nz
    chunks = tiles_x * tiles_y * freqs
    gx, gy, gz = lax.axis_index("gx"), lax.axis_index("gy"), lax.axis_index("sa")
    has_right, has_left = gx < nx - 1, gx > 0
    has_up, has_down = gy < ny - 1, gy > 0
    has_above, has_below = gz < nz - 1, gz > 0

    def split(j):
        return j // (tiles_y * freqs), (j // freqs) % tiles_y, j % freqs

    def chunk(slab, j):
        tx, ty, f = split(j)
        return own.at[tx, ty, f, slab]

    def load(j):
        tx, ty, f = split(j)
        return pltpu.make_async_copy(green.at[tx, ty, f], own.at[tx, ty, f, gz], load_sem.at[j])

    def remote(src, dst, send, recv, **where):
        return pltpu.make_async_remote_copy(
            src_ref=src, dst_ref=dst, send_sem=send, recv_sem=recv, device_id=where, device_id_type=MESH
        )

    def z_up(slab, j):
        here = chunk(slab, j)
        return remote(here, here, send_zu.at[slab, j], own_sem.at[slab, j], sa=gz + 1)

    def z_down(slab, j):
        here = chunk(slab, j)
        return remote(here, here, send_zd.at[slab, j], own_sem.at[slab, j], sa=gz - 1)

    def y_down(slab, tx, f):
        return remote(
            own.at[tx, 0, f, slab], up.at[tx, f, slab],
            send_yd.at[slab, tx, f], up_sem.at[slab, tx, f], gy=gy - 1,
        )

    def y_up(slab, tx, f):
        return remote(
            own.at[tx, tiles_y - 1, f, slab], down.at[tx, f, slab],
            send_yu.at[slab, tx, f], down_sem.at[slab, tx, f], gy=gy + 1,
        )

    def x_left(src, slab, row, f):
        return remote(
            src, right.at[row, f, slab], send_x.at[slab, row, f], right_sem.at[slab, row, f], gx=gx - 1
        )

    def each(count, body):
        def step(i, carry):
            body(i)
            return carry

        lax.fori_loop(0, count, step, 0)

    each(chunks, lambda j: load(j).start())

    barrier = pltpu.get_barrier_semaphore()
    sides = (
        (has_above, dict(sa=gz + 1)), (has_below, dict(sa=gz - 1)),
        (has_up, dict(gy=gy + 1)), (has_down, dict(gy=gy - 1)),
        (has_right, dict(gx=gx + 1)), (has_left, dict(gx=gx - 1)),
    )
    for there, where in sides:
        @pl.when(there)
        def _():
            pl.semaphore_signal(barrier, inc=1, device_id=where, device_id_type=MESH)
    pl.semaphore_wait(barrier, sum(there.astype(jnp.int32) for there, _ in sides))

    def pass_on(slab, j, upward, downward):
        tx, ty, f = split(j)
        if upward:
            pl.when(has_above)(lambda: z_up(slab, j).start())
        if downward:
            pl.when(has_below)(lambda: z_down(slab, j).start())
        pl.when((ty == 0) & has_down)(lambda: y_down(slab, tx, f).start())
        pl.when((ty == tiles_y - 1) & has_up)(lambda: y_up(slab, tx, f).start())
        pl.when((tx == 0) & has_left)(
            lambda: x_left(own.at[0, ty, f, slab], slab, ty + 1, f).start()
        )

    def halo(slab):
        def body(i):
            tx, f = i // freqs, i % freqs

            @pl.when(has_up)
            def _():
                y_down(slab, tx, f).wait_recv()
                pl.when((tx == 0) & has_left)(
                    lambda: x_left(up.at[0, f, slab], slab, tiles_y + 1, f).start()
                )

            @pl.when(has_down)
            def _():
                y_up(slab, tx, f).wait_recv()
                pl.when((tx == 0) & has_left)(
                    lambda: x_left(down.at[0, f, slab], slab, 0, f).start()
                )

        each(tiles_x * freqs, body)

        @pl.when(has_right)
        def _():
            def arrive(i):
                row, f = i // freqs, i % freqs

                def wait():
                    x_left(right.at[row, f, slab], slab, row, f).wait_recv()

                pl.when(((row > 0) | has_down) & ((row < tiles_y + 1) | has_up))(wait)

            each((tiles_y + 2) * freqs, arrive)

    lane = pl.multiple_of(gz * width // 128 * 128, 128)
    row_at = pl.multiple_of(gz * width % 128, width)

    def products(slab):
        def at_frequency(f):
            for tx in range(tiles_x):
                for ty in range(tiles_y):
                    for part in range(2):
                        turned[part] = own[tx, ty, f, slab, part, :, pl.ds(lane, 128)].T
                    real = turned[0, pl.ds(row_at, width), :]
                    imag = turned[1, pl.ds(row_at, width), :]
                    left[:width, :traces] = real
                    left[:width, traces:] = imag
                    left[width:, :traces] = -imag
                    left[width:, traces:] = real
                    for c, (dx, dy) in enumerate(CANDIDATES):
                        ox, oy = tx + dx, ty + dy
                        there = True
                        if ox == tiles_x:
                            there = has_right
                            beside = right.at[oy + 1, f, slab]
                        elif oy == tiles_y:
                            beside = up.at[ox, f, slab]
                        elif oy < 0:
                            beside = down.at[ox, f, slab]
                        else:
                            beside = own.at[ox, oy, f, slab]
                        if oy == tiles_y:
                            there = there & has_up
                        if oy < 0:
                            there = there & has_down

                        def add(beside=beside, c=c):
                            block = jnp.dot(
                                left[...], beside[...].reshape(2 * traces, points),
                                preferred_element_type=jnp.float32,
                            )
                            out[tx, ty, c, f, :, :points] += block[:width]
                            out[tx, ty, c, f, :, points:] += block[width:]

                        if there is True:
                            add()
                        else:
                            pl.when(there)(add)

        each(freqs, at_frequency)

    out[...] = jnp.zeros_like(out)

    for d in range(nz):
        if d == 0:
            def begin(j):
                load(j).wait()
                pass_on(gz, j, True, True)

            each(chunks, begin)
            halo(gz)
            products(gz)
        else:
            lower, upper = gz - d, gz + d

            def arrive(j):
                @pl.when(lower >= 0)
                def _():
                    z_up(lower, j).wait_recv()
                    pass_on(lower, j, True, False)

                @pl.when(upper < nz)
                def _():
                    z_down(upper, j).wait_recv()
                    pass_on(upper, j, False, True)

            each(chunks, arrive)
            for valid, slab in ((lower >= 0, lower), (upper < nz, upper)):
                @pl.when(valid)
                def _():
                    halo(slab)
                    products(slab)

    def finish(slab):
        def body(j):
            tx, ty, f = split(j)
            pl.when(has_above & (slab <= gz))(lambda: z_up(slab, j).wait_send())
            pl.when(has_below & (slab >= gz))(lambda: z_down(slab, j).wait_send())
            pl.when((ty == 0) & has_down)(lambda: y_down(slab, tx, f).wait_send())
            pl.when((ty == tiles_y - 1) & has_up)(lambda: y_up(slab, tx, f).wait_send())
            pl.when((tx == 0) & has_left)(
                lambda: x_left(own.at[0, ty, f, slab], slab, ty + 1, f).wait_send()
            )

        each(chunks, body)

        def edges(f):
            pl.when(has_up & has_left)(
                lambda: x_left(up.at[0, f, slab], slab, tiles_y + 1, f).wait_send()
            )
            pl.when(has_down & has_left)(
                lambda: x_left(down.at[0, f, slab], slab, 0, f).wait_send()
            )

        each(freqs, edges)

    each(nz, finish)


def per_device(green, offsets):
    tiles_x, tiles_y, freqs, _, traces, points = green.shape
    nx, ny, nz = (lax.axis_size(name) for name in ("gx", "gy", "sa"))
    width = points // nz
    chunks = tiles_x * tiles_y * freqs
    slabs = (nz, 2, traces, points)
    dma = pltpu.SemaphoreType.DMA
    blocks = pl.pallas_call(
        functools.partial(kernel, nx, ny, nz),
        out_shape=jax.ShapeDtypeStruct(
            (tiles_x, tiles_y, len(CANDIDATES), freqs, width, 2 * points), jnp.float32
        ),
        in_specs=[pl.BlockSpec(memory_space=pl.ANY)],
        out_specs=pl.BlockSpec(memory_space=pltpu.VMEM),
        scratch_shapes=[
            pltpu.VMEM((tiles_x, tiles_y, freqs) + slabs, jnp.bfloat16),
            pltpu.VMEM((tiles_x, freqs) + slabs, jnp.bfloat16),
            pltpu.VMEM((tiles_x, freqs) + slabs, jnp.bfloat16),
            pltpu.VMEM((tiles_y + 2, freqs) + slabs, jnp.bfloat16),
            pltpu.VMEM((2, 128, traces), jnp.bfloat16),
            pltpu.VMEM((2 * width, 2 * traces), jnp.bfloat16),
            dma((chunks,)),
            dma((nz, chunks)),
            dma((nz, tiles_x, freqs)),
            dma((nz, tiles_x, freqs)),
            dma((nz, tiles_y + 2, freqs)),
            dma((nz, chunks)),
            dma((nz, chunks)),
            dma((nz, tiles_x, freqs)),
            dma((nz, tiles_x, freqs)),
            dma((nz, tiles_y + 2, freqs)),
        ],
        compiler_params=pltpu.CompilerParams(
            collective_id=0, has_side_effects=True, vmem_limit_bytes=58 * 2**20
        ),
        cost_estimate=pl.CostEstimate(
            flops=2 * chunks * len(CANDIDATES) * width * 2 * points * 2 * traces * nz,
            bytes_accessed=12 * 2**20, transcendentals=0,
        ),
    )(green)
    dx, dy = offsets[:, 0], offsets[:, 1]
    wanted = jnp.where(dx == 0, dy, dy + 3)
    return jnp.stack(
        [lax.dynamic_index_in_dim(blocks, wanted[k], 2, keepdims=False) for k in range(offsets.shape[0])],
        axis=2,
    )


def solution(mesh):
    return jax.shard_map(
        per_device,
        mesh=mesh,
        in_specs=(P("gx", "gy", None, None, "sa", None), P()),
        out_specs=P("gx", "gy", None, None, "sa", None),
        check_vma=False,
    )
```

time: 444 us -> 174 us (0.39)
  waiting for transfers between devices: 304 us -> 0 us
  Pallas kernels: 0 us -> 156 us
  local copies, waits for them, and re-layouts: 61.3 us -> 3.41 us
  matrix products: 23.3 us -> 0 us
  between operations: 25.9 us -> 7.58 us
  other arithmetic: 17.7 us -> 3.34 us
  starting transfers between devices: 9.41 us -> 0 us
    reduce_scatter x1 -> x0, waiting for transfers between devices: 292 us -> none  [per_device(): return lax.psum_scatter(terms, 'sa', scatter_dimension=4, tiled=True)]
    pallas_call x0 -> x1, Pallas kernels: none -> 156 us  [per_device(): pl.pallas_call(functools.partial(kernel, nx, ny, nz), out_shape=jax.Shape...]
    dot_general x4 -> x0, matrix products: 23.3 us -> none  [pair_term(): jnp.einsum('nsp,nsq->npq', left, right, preferred_element_type=jnp.float32)]
    another operation x4 -> x0, local copies, waits for them, and re-layouts: 21 us -> none  [per_device(): terms = jnp.stack([pair_term(index) for index in range(NPAIR)], axis=2)]
    reshape x4 -> x0, local copies, waits for them, and re-layouts: 14.4 us -> none  [pair_term(): real_rows = beside.reshape(count, 2 * traces, points)]
    slice x7 -> x1, local copies, waits for them, and re-layouts: 13 us -> 0.66 us  [per_device(): wanted[k]]
    ppermute x3 -> x0, waiting for transfers between devices: 11.6 us -> none  [the longest x1 7.24 us: with_halo(): before = lax.ppermute(last, axis, up)]
    ppermute x3 -> x0, starting transfers between devices: 9.41 us -> none  [the longest x1 6.84 us: with_halo(): after = lax.ppermute(initial, axis, down)]
  transfers between devices with their start and end apart: 4 -> 0, of which waited for: 4 -> 0; matrix products, arithmetic and copies ran while one was open for 1% -> 0% of each run, Pallas kernels for 0% -> 0%
where the time goes in v1:
time: 174 us; the launch traced here: 170 us
  Pallas kernels  156 us (90%)
  between operations  7.58 us (4%)
  local copies, waits for them, and re-layouts  3.41 us (2%)
  other arithmetic  3.34 us (2%)
    pallas_call x1, Pallas kernels, per_device(): pl.pallas_call(functools.partial(kernel, nx, ny, nz), out_shape=jax.Shape...  156 us

profile of v1, /device:TPU:4, one launch (start us, length us, event | category | flops | bytes accessed | tf_op | source)
XLA Modules:
  0.0 170.2 jit_solution(16129265563327485114)
XLA Ops:
  0.0 0.8 bitcast_select_fusion
  0.8 0.7 fusion
  9.0 155.9 %shard_map.28 = f32[2,2,5,2,64,512]{5,4,3,2,1,0:T(8,128)} custom-call(bf16[2,2,2,2,256,256]{5,4,3,2,1,0:T(8,128)(2,1)} %green.1), custom_call_target="tpu_custom_call" | custom-call | flops 5368709120 | bytes 12582912 | tf_op jit(solution)/shard_map/pallas_call | solution.py:245
  164.9 2.8 %constant_dynamic-slice_fusion.3 = (f32[2,2,1,2,64,512]{5,4,3,2,1,0:T(8,128)S(1)}, f32[2,2,1,2,64,512]{5,4,3,2,1,0:T(8,128)S(1)}, f32[2,2,1,2,64,512]{5,4,3,2,1,0:T(8,128)S(1)}, f32[2,2,1,2,64,512]{5,4,3,2,1,0:T(8,128)S(1)}) fusion(f32[2,2,5,2,64,512]{5,4,3,2,1,0:T(8,128)} %shard_map.28, s32[]{:T(128)S(6)} %select_n.18, s32[]{:T(128)S(6)} %select_n.21, ...), kind=kLoop, calls=%fused_computation.5 | loop fusion | bytes 8388624 | tf_op jit(solution)/shard_map/jit(dynamic_index_in_dim)/dynamic_slice | solution.py:281
  167.6 2.6 %pad_maximum_fusion = f32[2,2,4,2,64,512]{5,4,3,2,1,0:T(8,128)} fusion(f32[2,2,1,2,64,512]{5,4,3,2,1,0:T(8,128)S(1)} %get-tuple-element.6, f32[2,2,1,2,64,512]{5,4,3,2,1,0:T(8,128)S(1)} %get-tuple-element.7, f32[2,2,1,2,64,512]{5,4,3,2,1,0:T(8,128)S(1)} %get-tuple-element.8, f32[2,2,1,2,64,512]{5,4,3,2,1,0:T(8,128)S(1)} %get-tuple-element.5), kind=kLoop, calls=%fused_computation | loop fusion | flops 3145728 | bytes 8388608 | tf_op jit(solution)/shard_map/stack | solution.py:280

commit v2 on v1

--- a/solution.py
+++ b/solution.py
@@ -12,20 +12,21 @@
 
 
 def kernel(
-    nx, ny, nz, green, out, own, up, down, right, turned, left,
+    nx, ny, nz, green, offsets, out, total, own, up, down, right, turned, left,
     load_sem, own_sem, up_sem, down_sem, right_sem,
     send_zu, send_zd, send_yu, send_yd, send_x,
 ):
     tiles_x, tiles_y, freqs, _, _, traces, points = own.shape
     width = points // nz
-    chunks = tiles_x * tiles_y * freqs
+    tiles = tiles_x * tiles_y
+    chunks = tiles * freqs
     gx, gy, gz = lax.axis_index("gx"), lax.axis_index("gy"), lax.axis_index("sa")
     has_right, has_left = gx < nx - 1, gx > 0
     has_up, has_down = gy < ny - 1, gy > 0
     has_above, has_below = gz < nz - 1, gz > 0
 
     def split(j):
-        return j // (tiles_y * freqs), (j // freqs) % tiles_y, j % freqs
+        return (j // tiles_y) % tiles_x, j % tiles_y, j // tiles
 
     def chunk(slab, j):
         tx, ty, f = split(j)
@@ -65,12 +66,12 @@
             src, right.at[row, f, slab], send_x.at[slab, row, f], right_sem.at[slab, row, f], gx=gx - 1
         )
 
-    def each(count, body):
+    def each(count, body, start=0):
         def step(i, carry):
             body(i)
             return carry
 
-        lax.fori_loop(0, count, step, 0)
+        lax.fori_loop(start, start + count, step, 0)
 
     each(chunks, lambda j: load(j).start())
 
@@ -98,10 +99,8 @@
             lambda: x_left(own.at[0, ty, f, slab], slab, ty + 1, f).start()
         )
 
-    def halo(slab):
-        def body(i):
-            tx, f = i // freqs, i % freqs
-
+    def halo(slab, f):
+        def body(tx):
             @pl.when(has_up)
             def _():
                 y_down(slab, tx, f).wait_recv()
@@ -116,81 +115,90 @@
                     lambda: x_left(down.at[0, f, slab], slab, 0, f).start()
                 )
 
-        each(tiles_x * freqs, body)
+        each(tiles_x, body)
 
         @pl.when(has_right)
         def _():
-            def arrive(i):
-                row, f = i // freqs, i % freqs
-
+            def arrive(row):
                 def wait():
                     x_left(right.at[row, f, slab], slab, row, f).wait_recv()
 
                 pl.when(((row > 0) | has_down) & ((row < tiles_y + 1) | has_up))(wait)
 
-            each((tiles_y + 2) * freqs, arrive)
+            each(tiles_y + 2, arrive)
 
     lane = pl.multiple_of(gz * width // 128 * 128, 128)
     row_at = pl.multiple_of(gz * width % 128, width)
 
-    def products(slab):
-        def at_frequency(f):
+    def products(slab, f):
+        for tx in range(tiles_x):
+            for ty in range(tiles_y):
+                for part in range(2):
+                    turned[part] = own[tx, ty, f, slab, part, :, pl.ds(lane, 128)].T
+                real = turned[0, pl.ds(row_at, width), :]
+                imag = turned[1, pl.ds(row_at, width), :]
+                left[:width, :traces] = real
+                left[:width, traces:] = imag
+                left[width:, :traces] = -imag
+                left[width:, traces:] = real
+                for c, (dx, dy) in enumerate(CANDIDATES):
+                    ox, oy = tx + dx, ty + dy
+                    there = True
+                    if ox == tiles_x:
+                        there = has_right
+                        beside = right.at[oy + 1, f, slab]
+                    elif oy == tiles_y:
+                        beside = up.at[ox, f, slab]
+                    elif oy < 0:
+                        beside = down.at[ox, f, slab]
+                    else:
+                        beside = own.at[ox, oy, f, slab]
+                    if oy == tiles_y:
+                        there = there & has_up
+                    if oy < 0:
+                        there = there & has_down
+
+                    def add(beside=beside, c=c):
+                        block = jnp.dot(
+                            left[...], beside[...].reshape(2 * traces, points),
+                            preferred_element_type=jnp.float32,
+                        )
+                        total[tx, ty, c, f, :, :points] += block[:width]
+                        total[tx, ty, c, f, :, points:] += block[width:]
+
+                    if there is True:
+                        add()
+                    else:
+                        pl.when(there)(add)
+
+    def select(f):
+        for k in range(offsets.shape[1]):
+            wanted = offsets[1, k] + 3 * offsets[0, k]
             for tx in range(tiles_x):
                 for ty in range(tiles_y):
-                    for part in range(2):
-                        turned[part] = own[tx, ty, f, slab, part, :, pl.ds(lane, 128)].T
-                    real = turned[0, pl.ds(row_at, width), :]
-                    imag = turned[1, pl.ds(row_at, width), :]
-                    left[:width, :traces] = real
-                    left[:width, traces:] = imag
-                    left[width:, :traces] = -imag
-                    left[width:, traces:] = real
-                    for c, (dx, dy) in enumerate(CANDIDATES):
-                        ox, oy = tx + dx, ty + dy
-                        there = True
-                        if ox == tiles_x:
-                            there = has_right
-                            beside = right.at[oy + 1, f, slab]
-                        elif oy == tiles_y:
-                            beside = up.at[ox, f, slab]
-                        elif oy < 0:
-                            beside = down.at[ox, f, slab]
-                        else:
-                            beside = own.at[ox, oy, f, slab]
-                        if oy == tiles_y:
-                            there = there & has_up
-                        if oy < 0:
-                            there = there & has_down
-
-                        def add(beside=beside, c=c):
-                            block = jnp.dot(
-                                left[...], beside[...].reshape(2 * traces, points),
-                                preferred_element_type=jnp.float32,
-                            )
-                            out[tx, ty, c, f, :, :points] += block[:width]
-                            out[tx, ty, c, f, :, points:] += block[width:]
-
-                        if there is True:
-                            add()
-                        else:
-                            pl.when(there)(add)
-
-        each(freqs, at_frequency)
-
-    out[...] = jnp.zeros_like(out)
-
-    for d in range(nz):
-        if d == 0:
-            def begin(j):
-                load(j).wait()
-                pass_on(gz, j, True, True)
-
-            each(chunks, begin)
-            halo(gz)
-            products(gz)
-        else:
-            lower, upper = gz - d, gz + d
-
+                    out[tx, ty, k, f] = total[tx, ty, wanted, f]
+
+    total[...] = jnp.zeros_like(total)
+
+    def take_own(f):
+        def begin(j):
+            load(j).wait()
+            pass_on(gz, j, True, True)
+
+        each(tiles, begin, f * tiles)
+
+    each(freqs, take_own)
+
+    def own_part(f):
+        halo(gz, f)
+        products(gz, f)
+
+    each(freqs, own_part)
+
+    for d in range(1, nz):
+        lower, upper = gz - d, gz + d
+
+        def further(f):
             def arrive(j):
                 @pl.when(lower >= 0)
                 def _():
@@ -202,12 +210,17 @@
                     z_down(upper, j).wait_recv()
                     pass_on(upper, j, False, True)
 
-            each(chunks, arrive)
+            each(tiles, arrive, f * tiles)
             for valid, slab in ((lower >= 0, lower), (upper < nz, upper)):
                 @pl.when(valid)
                 def _():
-                    halo(slab)
-                    products(slab)
+                    halo(slab, f)
+                    products(slab, f)
+
+            if d == nz - 1:
+                select(f)
+
+        each(freqs, further)
 
     def finish(slab):
         def body(j):
@@ -242,14 +255,17 @@
     chunks = tiles_x * tiles_y * freqs
     slabs = (nz, 2, traces, points)
     dma = pltpu.SemaphoreType.DMA
-    blocks = pl.pallas_call(
+    return pl.pallas_call(
         functools.partial(kernel, nx, ny, nz),
         out_shape=jax.ShapeDtypeStruct(
-            (tiles_x, tiles_y, len(CANDIDATES), freqs, width, 2 * points), jnp.float32
+            (tiles_x, tiles_y, offsets.shape[0], freqs, width, 2 * points), jnp.float32
         ),
-        in_specs=[pl.BlockSpec(memory_space=pl.ANY)],
+        in_specs=[pl.BlockSpec(memory_space=pl.ANY), pl.BlockSpec(memory_space=pltpu.SMEM)],
         out_specs=pl.BlockSpec(memory_space=pltpu.VMEM),
         scratch_shapes=[
+            pltpu.VMEM(
+                (tiles_x, tiles_y, len(CANDIDATES), freqs, width, 2 * points), jnp.float32
+            ),
             pltpu.VMEM((tiles_x, tiles_y, freqs) + slabs, jnp.bfloat16),
             pltpu.VMEM((tiles_x, freqs) + slabs, jnp.bfloat16),
             pltpu.VMEM((tiles_x, freqs) + slabs, jnp.bfloat16),
@@ -274,13 +290,7 @@
             flops=2 * chunks * len(CANDIDATES) * width * 2 * points * 2 * traces * nz,
             bytes_accessed=12 * 2**20, transcendentals=0,
         ),
-    )(green)
-    dx, dy = offsets[:, 0], offsets[:, 1]
-    wanted = jnp.where(dx == 0, dy, dy + 3)
-    return jnp.stack(
-        [lax.dynamic_index_in_dim(blocks, wanted[k], 2, keepdims=False) for k in range(offsets.shape[0])],
-        axis=2,
-    )
+    )(green, offsets.T)
 
 
 def solution(mesh):

time: 174 us -> 159 us (0.914); the launches traced: 170 us -> 159 us
  between operations: 7.58 us -> 0.01 us
  other arithmetic: 3.34 us -> 0 us
  Pallas kernels: 156 us -> 154 us
    unnamed x0 -> x1, local copies, waits for them, and re-layouts: none -> 4.91 us
    dynamic_slice x1 -> x0, local copies, waits for them, and re-layouts: 2.76 us -> none  [per_device(): lax.dynamic_index_in_dim(blocks, wanted[k], 2, keepdims=False)]
    another operation x1 -> x0, other arithmetic: 2.59 us -> none  [per_device(): jnp.stack([lax.dynamic_index_in_dim(blocks, wanted[k], 2, keepdims=False)...]
    pallas_call x1, Pallas kernels: 156 us -> 154 us  [per_device(): pl.pallas_call(functools.partial(kernel, nx, ny, nz), out_shape=jax.Shape...]
where the time goes in v2:
time: 159 us
  Pallas kernels  154 us (97%)
  local copies, waits for them, and re-layouts  4.91 us (3%)
    pallas_call x1, Pallas kernels, per_device(): pl.pallas_call(functools.partial(kernel, nx, ny, nz), out_shape=jax.Shape...  154 us
    unnamed x1, local copies, waits for them, and re-layouts  4.91 us

profile of v2, /device:TPU:4, one launch (start us, length us, event | category | flops | bytes accessed | tf_op | source)
XLA Modules:
  0.0 158.9 jit_solution(14771455614104026604)
XLA Ops:
  0.0 153.9 %shard_map.28 = f32[2,2,4,2,64,512]{5,4,3,2,1,0:T(8,128)} custom-call(bf16[2,2,2,2,256,256]{5,4,3,2,1,0:T(8,128)(2,1)} %green.1, s32[2,4]{1,0:T(2,128)} %bitcast.1), custom_call_target="tpu_custom_call" | custom-call | flops 5368709120 | bytes 12582912 | tf_op jit(solution)/shard_map/pallas_call | solution.py:258
  153.9 4.9 %copy.4 = f32[2,2,4,2,64,512]{5,4,3,2,1,0:T(8,128)} copy(f32[2,2,4,2,64,512]{5,4,3,2,1,0:T(8,128)} %shard_map.28) | data formatting | bytes 8388608

commit v3 on v0

v3 whole, which is shorter than its diff:
```python
import functools

import jax
import jax.numpy as jnp
from jax import lax
from jax.experimental import pallas as pl
from jax.experimental.pallas import tpu as pltpu
from jax.sharding import PartitionSpec as P

MESH = pl.DeviceIdType.MESH
CANDIDATES = ((0, 0), (0, 1), (1, -1), (1, 0), (1, 1))


def kernel(
    nx, ny, nz, green, offsets, out, total, beyond, stage, own, up, down, right, turned, left,
    load_sem, own_sem, up_sem, down_sem, right_sem, end_sem,
    send_zu, send_zd, send_yu, send_yd, send_x, send_end,
):
    freqs, _, halves, tiles_x, tiles_y, _, traces, lanes = own.shape
    points = halves * lanes
    width = points // nz
    phases = halves * freqs
    pairs = offsets.shape[1]
    gx, gy, gz = lax.axis_index("gx"), lax.axis_index("gy"), lax.axis_index("sa")
    has_right, has_left = gx < nx - 1, gx > 0
    has_up, has_down = gy < ny - 1, gy > 0
    has_above, has_below = gz < nz - 1, gz > 0
    inside = has_above & has_below
    raw_up, raw_down = gz < nz - 2, gz > 1
    near_top, near_bottom = gz == nz - 2, gz == 1
    near = near_top | near_bottom
    beside_end = jnp.where(near_top, gz + 1, gz - 1)

    def remote(src, dst, send, recv, **where):
        return pltpu.make_async_remote_copy(
            src_ref=src, dst_ref=dst, send_sem=send, recv_sem=recv, device_id=where, device_id_type=MESH
        )

    def load(f, h):
        columns = pl.ds(pl.multiple_of(h * lanes, lanes), lanes)
        return pltpu.make_async_copy(
            green.at[:, :, f, :, :, columns], own.at[f, gz, h], load_sem.at[f, h]
        )

    def z_up(f, slab, h):
        here = own.at[f, slab, h]
        return remote(here, here, send_zu.at[f, slab, h], own_sem.at[f, slab, h], sa=gz + 1)

    def z_down(f, slab, h):
        here = own.at[f, slab, h]
        return remote(here, here, send_zd.at[f, slab, h], own_sem.at[f, slab, h], sa=gz - 1)

    def y_down(f, slab, h):
        return remote(
            own.at[f, slab, h, :, 0], up.at[f, slab, h],
            send_yd.at[f, slab, h], up_sem.at[f, slab, h], gy=gy - 1,
        )

    def y_up(f, slab, h):
        return remote(
            own.at[f, slab, h, :, tiles_y - 1], down.at[f, slab, h],
            send_yu.at[f, slab, h], down_sem.at[f, slab, h], gy=gy + 1,
        )

    def x_left(kind, f, slab, h):
        src, dst = (
            (own.at[f, slab, h, 0], right.at[f, slab, h, pl.ds(1, tiles_y)]),
            (up.at[f, slab, h, 0], right.at[f, slab, h, tiles_y + 1]),
            (down.at[f, slab, h, 0], right.at[f, slab, h, 0]),
        )[kind]
        return remote(
            src, dst, send_x.at[kind, f, slab, h], right_sem.at[kind, f, slab, h], gx=gx - 1
        )

    def to_end(f, h, part):
        columns = pl.ds(pl.multiple_of(part * points + h * lanes, lanes), lanes)
        return remote(
            stage.at[:, :, :, f, :, columns], out.at[:, :, :, f, :, columns],
            send_end.at[f, h, part], end_sem.at[f, h, part], sa=beside_end,
        )

    def each(count, body, start=0):
        def step(i, carry):
            body(i)
            return carry

        lax.fori_loop(start, count, step, 0)

    def each_half(body):
        each(phases, lambda u: body(u // halves, u % halves))

    each_half(lambda f, h: load(f, h).start())

    barrier = pltpu.get_barrier_semaphore()
    sides = (
        (has_above, dict(sa=gz + 1)), (has_below, dict(sa=gz - 1)),
        (has_up, dict(gy=gy + 1)), (has_down, dict(gy=gy - 1)),
        (has_right, dict(gx=gx + 1)), (has_left, dict(gx=gx - 1)),
    )
    for there, where in sides:
        @pl.when(there)
        def _():
            pl.semaphore_signal(barrier, inc=1, device_id=where, device_id_type=MESH)
    pl.semaphore_wait(barrier, sum(there.astype(jnp.int32) for there, _ in sides))

    def push(f, slab, h):
        pl.when(has_down)(lambda: y_down(f, slab, h).start())
        pl.when(has_up)(lambda: y_up(f, slab, h).start())
        pl.when(has_left)(lambda: x_left(0, f, slab, h).start())

    def halo(f, slab, h):
        @pl.when(has_up)
        def _():
            y_down(f, slab, h).wait_recv()
            pl.when(has_left)(lambda: x_left(1, f, slab, h).start())

        @pl.when(has_down)
        def _():
            y_up(f, slab, h).wait_recv()
            pl.when(has_left)(lambda: x_left(2, f, slab, h).start())

        @pl.when(has_right)
        def _():
            x_left(0, f, slab, h).wait_recv()
            pl.when(has_up)(lambda: x_left(1, f, slab, h).wait_recv())
            pl.when(has_down)(lambda: x_left(2, f, slab, h).wait_recv())

    def send_own(u):
        f, v = u // halves, u % halves
        pl.when(raw_up)(lambda: z_up(f, gz, 1 - v).start())
        pl.when(raw_down)(lambda: z_down(f, gz, v).start())

    mine = gz * width // lanes
    row_at = pl.multiple_of(gz * width % lanes, width)
    row_beyond = pl.multiple_of(beside_end * width % lanes, width)

    def products(f, slab, h, both):
        rows = 4 * width if both else 2 * width
        for tx in range(tiles_x):
            for ty in range(tiles_y):
                for part in range(2):
                    turned[part] = own[f, slab, mine, tx, ty, part].T
                for base, start in ((0, row_at), (2 * width, row_beyond))[: 2 if both else 1]:
                    real = turned[0, pl.ds(start, width), :]
                    imag = turned[1, pl.ds(start, width), :]
                    left[base : base + width, :traces] = real
                    left[base : base + width, traces:] = imag
                    left[base + width : base + 2 * width, :traces] = -imag
                    left[base + width : base + 2 * width, traces:] = real
                for c, (dx, dy) in enumerate(CANDIDATES):
                    ox, oy = tx + dx, ty + dy
                    there = True
                    if ox == tiles_x:
                        there = has_right
                        beside = right.at[f, slab, h, oy + 1]
                    elif oy == tiles_y:
                        beside = up.at[f, slab, h, ox]
                    elif oy < 0:
                        beside = down.at[f, slab, h, ox]
                    else:
                        beside = own.at[f, slab, h, ox, oy]
                    if oy == tiles_y:
                        there = there & has_up
                    if oy < 0:
                        there = there & has_down

                    def add(beside=beside, c=c):
                        block = jnp.dot(
                            left[:rows], beside[...].reshape(2 * traces, lanes),
                            preferred_element_type=jnp.float32,
                        )
                        total[f, tx, ty, c, h, :, :lanes] += block[:width]
                        total[f, tx, ty, c, h, :, lanes:] += block[width : 2 * width]
                        if both:
                            beyond[f, tx, ty, c, h, :, :lanes] += block[2 * width : 3 * width]
                            beyond[f, tx, ty, c, h, :, lanes:] += block[3 * width :]

                    if there is True:
                        add()
                    else:
                        pl.when(there)(add)

    def choose(f, h, source, target, add):
        for k in range(pairs):
            wanted = offsets[1, k] + 3 * offsets[0, k]
            for tx in range(tiles_x):
                for ty in range(tiles_y):
                    for part in range(2):
                        columns = pl.ds(pl.multiple_of(part * points + h * lanes, lanes), lanes)
                        value = source[f, tx, ty, wanted, h, :, part * lanes : (part + 1) * lanes]
                        if add:
                            value = value + target[tx, ty, k, f, :, columns]
                        target[tx, ty, k, f, :, columns] = value

    def take(f, h):
        load(f, h).wait()
        push(f, gz, h)

    each(halves, lambda h: load(0, h).wait())
    send_own(0)
    each(halves, lambda h: push(0, gz, h))
    each(phases, lambda u: take(u // halves, u % halves), halves)
    total[...] = jnp.zeros_like(total)

    @pl.when(jnp.logical_not(inside))
    def _():
        each(phases, send_own, 1)

        def own_part(f, h):
            halo(f, gz, h)
            products(f, gz, h, False)

        each_half(own_part)

        def receive(f, v):
            h = jnp.where(gz == 0, v, 1 - v)
            for part in range(2):
                to_end(f, h, part).wait_recv()
            choose(f, h, total, out, True)

        each_half(receive)

    @pl.when(inside)
    def _():
        beyond[...] = jnp.zeros_like(beyond)

        def phase(f, v):
            u = f * halves + v
            near_h = jnp.where(near_top, 1 - v, v)

            def at(d):
                lower, upper = gz - d, gz + d

                @pl.when(lower >= 0)
                def _():
                    z_up(f, lower, 1 - v).wait_recv()
                    pl.when(raw_up)(lambda: z_up(f, lower, 1 - v).start())
                    push(f, lower, 1 - v)

                @pl.when(upper < nz)
                def _():
                    z_down(f, upper, v).wait_recv()
                    pl.when(raw_down)(lambda: z_down(f, upper, v).start())
                    push(f, upper, v)

                pl.when((d == 1) & (u + 1 < phases))(lambda: send_own(u + 1))

                @pl.when((d == 1) & (v == 0) & near)
                def _():
                    def own_part(h):
                        halo(f, gz, h)
                        products(f, gz, h, True)

                    each(halves, own_part)

                slab = jnp.where(near_top, lower, upper)

                @pl.when(near & (slab >= 0) & (slab < nz))
                def _():
                    halo(f, slab, near_h)
                    products(f, slab, near_h, True)

            each(nz, at, 1)

            @pl.when(near)
            def _():
                choose(f, near_h, beyond, stage, False)
                for part in range(2):
                    to_end(f, near_h, part).start()

            @pl.when(v == halves - 1)
            def _():
                def rest(slab):
                    done = (near_top & (slab <= gz)) | (near_bottom & (slab >= gz))

                    @pl.when(jnp.logical_not(done))
                    def _():
                        def part(h):
                            halo(f, slab, h)
                            products(f, slab, h, False)

                        each(halves, part)

                each(nz, rest)
                each(halves, lambda h: choose(f, h, total, out, False))

        each_half(phase)

    def finish(slab):
        def body(f, h):
            pl.when(raw_up & (slab <= gz))(lambda: z_up(f, slab, h).wait_send())
            pl.when(raw_down & (slab >= gz))(lambda: z_down(f, slab, h).wait_send())

            @pl.when(inside | (slab == gz))
            def _():
                pl.when(has_down)(lambda: y_down(f, slab, h).wait_send())
                pl.when(has_up)(lambda: y_up(f, slab, h).wait_send())

                @pl.when(has_left)
                def _():
                    x_left(0, f, slab, h).wait_send()
                    pl.when(has_up)(lambda: x_left(1, f, slab, h).wait_send())
                    pl.when(has_down)(lambda: x_left(2, f, slab, h).wait_send())

        each_half(body)

    each(nz, finish)

    @pl.when(near)
    def _():
        def body(f, h):
            for part in range(2):
                to_end(f, h, part).wait_send()

        each_half(body)


def per_device(green, offsets):
    tiles_x, tiles_y, freqs, _, traces, points = green.shape
    nx, ny, nz = (lax.axis_size(name) for name in ("gx", "gy", "sa"))
    width, lanes, pairs = points // nz, 128, offsets.shape[0]
    halves = points // lanes
    dma = pltpu.SemaphoreType.DMA
    result = (tiles_x, tiles_y, pairs, freqs, width, 2 * points)
    sums = (freqs, tiles_x, tiles_y, len(CANDIDATES), halves, width, 2 * lanes)
    piece, cell = (freqs, nz, halves), (2, traces, lanes)
    return pl.pallas_call(
        functools.partial(kernel, nx, ny, nz),
        out_shape=jax.ShapeDtypeStruct(result, jnp.float32),
        in_specs=[pl.BlockSpec(memory_space=pl.ANY), pl.BlockSpec(memory_space=pltpu.SMEM)],
        out_specs=pl.BlockSpec(memory_space=pltpu.VMEM),
        scratch_shapes=[
            pltpu.VMEM(sums, jnp.float32),
            pltpu.VMEM(sums, jnp.float32),
            pltpu.VMEM(result, jnp.float32),
            pltpu.VMEM(piece + (tiles_x, tiles_y) + cell, jnp.bfloat16),
            pltpu.VMEM(piece + (tiles_x,) + cell, jnp.bfloat16),
            pltpu.VMEM(piece + (tiles_x,) + cell, jnp.bfloat16),
            pltpu.VMEM(piece + (tiles_y + 2,) + cell, jnp.bfloat16),
            pltpu.VMEM((2, lanes, traces), jnp.bfloat16),
            pltpu.VMEM((4 * width, 2 * traces), jnp.bfloat16),
            dma((freqs, halves)),
            dma(piece),
            dma(piece),
            dma(piece),
            dma((3,) + piece),
            dma((freqs, halves, 2)),
            dma(piece),
            dma(piece),
            dma(piece),
            dma(piece),
            dma((3,) + piece),
            dma((freqs, halves, 2)),
        ],
        compiler_params=pltpu.CompilerParams(
            collective_id=0, has_side_effects=True, vmem_limit_bytes=61 * 2**20
        ),
        cost_estimate=pl.CostEstimate(
            flops=2 * tiles_x * tiles_y * freqs * len(CANDIDATES) * width * 2 * points * 2 * traces * nz,
            bytes_accessed=12 * 2**20, transcendentals=0,
        ),
    )(green, offsets.T)


def solution(mesh):
    return jax.shard_map(
        per_device,
        mesh=mesh,
        in_specs=(P("gx", "gy", None, None, "sa", None), P()),
        out_specs=P("gx", "gy", None, None, "sa", None),
        check_vma=False,
    )
```

time: 444 us -> 164 us (0.37)
  waiting for transfers between devices: 304 us -> 0 us
  Pallas kernels: 0 us -> 157 us
  local copies, waits for them, and re-layouts: 61.3 us -> 4.91 us
  between operations: 25.9 us -> 0.01 us
  matrix products: 23.3 us -> 0 us
  other arithmetic: 17.7 us -> 0 us
  starting transfers between devices: 9.41 us -> 0 us
    reduce_scatter x1 -> x0, waiting for transfers between devices: 292 us -> none  [per_device(): return lax.psum_scatter(terms, 'sa', scatter_dimension=4, tiled=True)]
    pallas_call x0 -> x1, Pallas kernels: none -> 157 us  [per_device(): pl.pallas_call(functools.partial(kernel, nx, ny, nz), out_shape=jax.Shape...]
    dot_general x4 -> x0, matrix products: 23.3 us -> none  [pair_term(): jnp.einsum('nsp,nsq->npq', left, right, preferred_element_type=jnp.float32)]
    another operation x4 -> x0, local copies, waits for them, and re-layouts: 21 us -> none  [per_device(): terms = jnp.stack([pair_term(index) for index in range(NPAIR)], axis=2)]
    reshape x4 -> x0, local copies, waits for them, and re-layouts: 14.4 us -> none  [pair_term(): real_rows = beside.reshape(count, 2 * traces, points)]
    slice x7 -> x0, local copies, waits for them, and re-layouts: 13 us -> none  [the longest x4 9.15 us: pair_term(): beside[:, :, :, 1]]
    another operation x1 -> x0, other arithmetic: 11.6 us -> none  [per_device(): terms = jnp.stack([pair_term(index) for index in range(NPAIR)], axis=2)]
    ppermute x3 -> x0, waiting for transfers between devices: 11.6 us -> none  [the longest x1 7.24 us: with_halo(): before = lax.ppermute(last, axis, up)]
  transfers between devices with their start and end apart: 4 -> 0, of which waited for: 4 -> 0; matrix products, arithmetic and copies ran while one was open for 1% -> 0% of each run, Pallas kernels for 0% -> 0%
where the time goes in v3:
time: 164 us; the launch traced here: 162 us
  Pallas kernels  157 us (96%)
  local copies, waits for them, and re-layouts  4.91 us (3%)
    pallas_call x1, Pallas kernels, per_device(): pl.pallas_call(functools.partial(kernel, nx, ny, nz), out_shape=jax.Shape...  157 us
    unnamed x1, local copies, waits for them, and re-layouts  4.91 us

profile of v3, /device:TPU:4, one launch (start us, length us, event | category | flops | bytes accessed | tf_op | source)
XLA Modules:
  0.0 161.9 jit_solution(1076535979197755814)
XLA Ops:
  0.0 156.9 %shard_map.28 = f32[2,2,4,2,64,512]{5,4,3,2,1,0:T(8,128)} custom-call(bf16[2,2,2,2,256,256]{5,4,3,2,1,0:T(8,128)(2,1)} %green.1, s32[2,4]{1,0:T(2,128)} %bitcast.1), custom_call_target="tpu_custom_call" | custom-call | flops 5368709120 | bytes 12582912 | tf_op jit(solution)/shard_map/pallas_call | solution.py:327
  156.9 4.9 %copy.4 = f32[2,2,4,2,64,512]{5,4,3,2,1,0:T(8,128)} copy(f32[2,2,4,2,64,512]{5,4,3,2,1,0:T(8,128)} %shard_map.28) | data formatting | bytes 8388608

commit v4 on v3

--- a/solution.py
+++ b/solution.py
@@ -14,7 +14,7 @@
 def kernel(
     nx, ny, nz, green, offsets, out, total, beyond, stage, own, up, down, right, turned, left,
     load_sem, own_sem, up_sem, down_sem, right_sem, end_sem,
-    send_zu, send_zd, send_yu, send_yd, send_x, send_end,
+    send_zu, send_zd, send_yu, send_yd, send_x, send_end, send_halo,
 ):
     freqs, _, halves, tiles_x, tiles_y, _, traces, lanes = own.shape
     points = halves * lanes
@@ -29,7 +29,10 @@
     raw_up, raw_down = gz < nz - 2, gz > 1
     near_top, near_bottom = gz == nz - 2, gz == 1
     near = near_top | near_bottom
+    at_end = jnp.logical_not(inside)
+    middle = inside & jnp.logical_not(near)
     beside_end = jnp.where(near_top, gz + 1, gz - 1)
+    inward = jnp.where(has_below, gz - 1, gz + 1)
 
     def remote(src, dst, send, recv, **where):
         return pltpu.make_async_remote_copy(
@@ -78,6 +81,14 @@
             stage.at[:, :, :, f, :, columns], out.at[:, :, :, f, :, columns],
             send_end.at[f, h, part], end_sem.at[f, h, part], sa=beside_end,
         )
+
+    def halo_up(f, h):
+        here = up.at[f, gz, h]
+        return remote(here, here, send_halo.at[0, f, h], up_sem.at[f, gz, h], sa=inward)
+
+    def halo_down(f, h):
+        here = down.at[f, gz, h]
+        return remote(here, here, send_halo.at[1, f, h], down_sem.at[f, gz, h], sa=inward)
 
     def each(count, body, start=0):
         def step(i, carry):
@@ -103,12 +114,15 @@
             pl.semaphore_signal(barrier, inc=1, device_id=where, device_id_type=MESH)
     pl.semaphore_wait(barrier, sum(there.astype(jnp.int32) for there, _ in sides))
 
+    def push_x(f, slab, h):
+        pl.when(has_left)(lambda: x_left(0, f, slab, h).start())
+
     def push(f, slab, h):
         pl.when(has_down)(lambda: y_down(f, slab, h).start())
         pl.when(has_up)(lambda: y_up(f, slab, h).start())
-        pl.when(has_left)(lambda: x_left(0, f, slab, h).start())
-
-    def halo(f, slab, h):
+        push_x(f, slab, h)
+
+    def halo_y(f, slab, h):
         @pl.when(has_up)
         def _():
             y_down(f, slab, h).wait_recv()
@@ -119,6 +133,7 @@
             y_up(f, slab, h).wait_recv()
             pl.when(has_left)(lambda: x_left(2, f, slab, h).start())
 
+    def halo_x(f, slab, h):
         @pl.when(has_right)
         def _():
             x_left(0, f, slab, h).wait_recv()
@@ -192,22 +207,40 @@
                             value = value + target[tx, ty, k, f, :, columns]
                         target[tx, ty, k, f, :, columns] = value
 
-    def take(f, h):
-        load(f, h).wait()
-        push(f, gz, h)
+    def rest(f, slab):
+        each(halves, lambda h: halo_y(f, slab, h))
+
+        def part(h):
+            halo_x(f, slab, h)
+            products(f, slab, h, False)
+
+        each(halves, part)
 
     each(halves, lambda h: load(0, h).wait())
     send_own(0)
-    each(halves, lambda h: push(0, gz, h))
-    each(phases, lambda u: take(u // halves, u % halves), halves)
-    total[...] = jnp.zeros_like(total)
-
-    @pl.when(jnp.logical_not(inside))
+
+    @pl.when(near)
+    def _():
+        push(0, gz, jnp.where(near_top, 1, 0))
+
+    each(phases, lambda u: load(u // halves, u % halves).wait(), halves)
+
+    @pl.when(at_end)
     def _():
         each(phases, send_own, 1)
+        each_half(lambda f, v: push(f, gz, jnp.where(gz == 0, v, 1 - v)))
+        total[...] = jnp.zeros_like(total)
+
+        def pass_halo(f, v):
+            h = jnp.where(gz == 0, v, 1 - v)
+            halo_y(f, gz, h)
+            pl.when(has_up)(lambda: halo_up(f, h).start())
+            pl.when(has_down)(lambda: halo_down(f, h).start())
+
+        each_half(pass_halo)
 
         def own_part(f, h):
-            halo(f, gz, h)
+            halo_x(f, gz, h)
             products(f, gz, h, False)
 
         each_half(own_part)
@@ -220,81 +253,132 @@
 
         each_half(receive)
 
-    @pl.when(inside)
+    @pl.when(near)
     def _():
+        end = beside_end
+
+        def pass_end(u):
+            f, v = u // halves, u % halves
+
+            @pl.when(near_top)
+            def _():
+                z_down(f, end, v).wait_recv()
+                z_down(f, end, v).start()
+                push_x(f, end, v)
+
+            @pl.when(near_bottom)
+            def _():
+                z_up(f, end, 1 - v).wait_recv()
+                z_up(f, end, 1 - v).start()
+                push_x(f, end, 1 - v)
+
+            pl.when(u + 1 < phases)(lambda: send_own(u + 1))
+
+        total[...] = jnp.zeros_like(total)
         beyond[...] = jnp.zeros_like(beyond)
+        pass_end(0)
 
         def phase(f, v):
             u = f * halves + v
-            near_h = jnp.where(near_top, 1 - v, v)
+            h = jnp.where(near_top, 1 - v, v)
 
             def at(d):
-                lower, upper = gz - d, gz + d
-
-                @pl.when(lower >= 0)
-                def _():
-                    z_up(f, lower, 1 - v).wait_recv()
-                    pl.when(raw_up)(lambda: z_up(f, lower, 1 - v).start())
-                    push(f, lower, 1 - v)
-
-                @pl.when(upper < nz)
-                def _():
-                    z_down(f, upper, v).wait_recv()
-                    pl.when(raw_down)(lambda: z_down(f, upper, v).start())
-                    push(f, upper, v)
-
-                pl.when((d == 1) & (u + 1 < phases))(lambda: send_own(u + 1))
-
-                @pl.when((d == 1) & (v == 0) & near)
-                def _():
-                    def own_part(h):
-                        halo(f, gz, h)
-                        products(f, gz, h, True)
-
-                    each(halves, own_part)
-
-                slab = jnp.where(near_top, lower, upper)
-
-                @pl.when(near & (slab >= 0) & (slab < nz))
-                def _():
-                    halo(f, slab, near_h)
-                    products(f, slab, near_h, True)
-
-            each(nz, at, 1)
-
-            @pl.when(near)
-            def _():
-                choose(f, near_h, beyond, stage, False)
-                for part in range(2):
-                    to_end(f, near_h, part).start()
-
-            @pl.when(v == halves - 1)
-            def _():
-                def rest(slab):
-                    done = (near_top & (slab <= gz)) | (near_bottom & (slab >= gz))
-
-                    @pl.when(jnp.logical_not(done))
+                slab = jnp.where(near_top, gz - d, gz + d)
+
+                @pl.when(near_top)
+                def _():
+                    z_up(f, slab, h).wait_recv()
+
+                @pl.when(near_bottom)
+                def _():
+                    z_down(f, slab, h).wait_recv()
+
+                push(f, slab, h)
+                pl.when((d == 2) & (u + 1 < phases))(lambda: pass_end(u + 1))
+
+                @pl.when(d == 1)
+                def _():
+                    halo_y(f, gz, h)
+
+                halo_y(f, slab, h)
+
+                def work(slab):
+                    halo_x(f, slab, h)
+                    products(f, slab, h, True)
+
+                @pl.when((d == 1) & (v == halves - 1) & (f > 0))
+                def _():
+                    rest(f - 1, end)
+                    each(halves, lambda i: choose(f - 1, i, total, out, False))
+
+                each(jnp.where(d == 1, 2, 1), lambda i: work(jnp.where((d == 1) & (i == 0), gz, slab)))
+
+                @pl.when((d == 1) & (u + 1 < phases))
+                def _():
+                    later = (u + 1) % halves
+                    push((u + 1) // halves, gz, jnp.where(near_top, 1 - later, later))
+
+            each(nz - 1, at, 1)
+            choose(f, h, beyond, stage, False)
+            for part in range(2):
+                to_end(f, h, part).start()
+
+        each_half(phase)
+        rest(freqs - 1, end)
+        each(halves, lambda h: choose(freqs - 1, h, total, out, False))
+
+    if nz > 4:
+        @pl.when(middle)
+        def _():
+            each_half(lambda f, h: push(f, gz, h))
+            total[...] = jnp.zeros_like(total)
+
+            def phase(f, v):
+                u = f * halves + v
+
+                def at(d):
+                    lower, upper = gz - d, gz + d
+
+                    @pl.when(lower >= 0)
                     def _():
-                        def part(h):
-                            halo(f, slab, h)
-                            products(f, slab, h, False)
-
-                        each(halves, part)
-
-                each(nz, rest)
-                each(halves, lambda h: choose(f, h, total, out, False))
-
-        each_half(phase)
+                        z_up(f, lower, 1 - v).wait_recv()
+                        z_up(f, lower, 1 - v).start()
+                        push(f, lower, 1 - v)
+
+                    @pl.when(upper < nz)
+                    def _():
+                        z_down(f, upper, v).wait_recv()
+                        z_down(f, upper, v).start()
+                        push(f, upper, v)
+
+                    pl.when((d == 1) & (u + 1 < phases))(lambda: send_own(u + 1))
+
+                each(nz, at, 1)
+
+                @pl.when(v == halves - 1)
+                def _():
+                    each(nz, lambda slab: rest(f, slab))
+                    each(halves, lambda h: choose(f, h, total, out, False))
+
+            each_half(phase)
 
     def finish(slab):
         def body(f, h):
             pl.when(raw_up & (slab <= gz))(lambda: z_up(f, slab, h).wait_send())
             pl.when(raw_down & (slab >= gz))(lambda: z_down(f, slab, h).wait_send())
 
-            @pl.when(inside | (slab == gz))
+            @pl.when(middle | (slab == gz) | (near & (slab != beside_end)))
             def _():
                 pl.when(has_down)(lambda: y_down(f, slab, h).wait_send())
                 pl.when(has_up)(lambda: y_up(f, slab, h).wait_send())
+
+            @pl.when(at_end & (slab == gz))
+            def _():
+                pl.when(has_up)(lambda: halo_up(f, h).wait_send())
+                pl.when(has_down)(lambda: halo_down(f, h).wait_send())
+
+            @pl.when(inside | (slab == gz))
+            def _():
 
                 @pl.when(has_left)
                 def _():
@@ -351,6 +435,7 @@
             dma(piece),
             dma((3,) + piece),
             dma((freqs, halves, 2)),
+            dma((2, freqs, halves)),
         ],
         compiler_params=pltpu.CompilerParams(
             collective_id=0, has_side_effects=True, vmem_limit_bytes=61 * 2**20

time: 164 us -> 161 us (0.982); the launches traced: 162 us -> 161 us
  no operation moved by 1% of the time
where the time goes in v4:
time: 161 us
  Pallas kernels  156 us (97%)
  local copies, waits for them, and re-layouts  4.91 us (3%)
    pallas_call x1, Pallas kernels, per_device(): pl.pallas_call(functools.partial(kernel, nx, ny, nz), out_shape=jax.Shape...  156 us
    unnamed x1, local copies, waits for them, and re-layouts  4.91 us

profile of v4, /device:TPU:4, one launch (start us, length us, event | category | flops | bytes accessed | tf_op | source)
XLA Modules:
  0.0 161.0 jit_solution(902912833676617907)
XLA Ops:
  0.0 156.0 %shard_map.28 = f32[2,2,4,2,64,512]{5,4,3,2,1,0:T(8,128)} custom-call(bf16[2,2,2,2,256,256]{5,4,3,2,1,0:T(8,128)(2,1)} %green.1, s32[2,4]{1,0:T(2,128)} %bitcast.1), custom_call_target="tpu_custom_call" | custom-call | flops 5368709120 | bytes 12582912 | tf_op jit(solution)/shard_map/pallas_call | solution.py:411
  156.1 4.9 %copy.4 = f32[2,2,4,2,64,512]{5,4,3,2,1,0:T(8,128)} copy(f32[2,2,4,2,64,512]{5,4,3,2,1,0:T(8,128)} %shard_map.28) | data formatting | bytes 8388608

commit v5 on v4

--- a/solution.py
+++ b/solution.py
@@ -276,11 +276,29 @@
 
         total[...] = jnp.zeros_like(total)
         beyond[...] = jnp.zeros_like(beyond)
+
+        def near_half(v):
+            return jnp.where(near_top, 1 - v, v)
+
+        def work(f, slab, h):
+            halo_y(f, slab, h)
+            halo_x(f, slab, h)
+            products(f, slab, h, True)
+
+        work(0, gz, near_half(0))
         pass_end(0)
+
+        def rest_half(f, v):
+            h = jnp.where(near_top, v, 1 - v)
+            halo_y(f, end, h)
+            halo_x(f, end, h)
+            products(f, end, h, False)
 
         def phase(f, v):
             u = f * halves + v
-            h = jnp.where(near_top, 1 - v, v)
+            more = u + 1 < phases
+            h = near_half(v)
+            next_f, next_h = (u + 1) // halves, near_half((u + 1) % halves)
 
             def at(d):
                 slab = jnp.where(near_top, gz - d, gz + d)
@@ -294,37 +312,32 @@
                     z_down(f, slab, h).wait_recv()
 
                 push(f, slab, h)
-                pl.when((d == 2) & (u + 1 < phases))(lambda: pass_end(u + 1))
-
-                @pl.when(d == 1)
-                def _():
-                    halo_y(f, gz, h)
-
-                halo_y(f, slab, h)
-
-                def work(slab):
-                    halo_x(f, slab, h)
-                    products(f, slab, h, True)
-
-                @pl.when((d == 1) & (v == halves - 1) & (f > 0))
-                def _():
-                    rest(f - 1, end)
-                    each(halves, lambda i: choose(f - 1, i, total, out, False))
-
-                each(jnp.where(d == 1, 2, 1), lambda i: work(jnp.where((d == 1) & (i == 0), gz, slab)))
-
-                @pl.when((d == 1) & (u + 1 < phases))
-                def _():
-                    later = (u + 1) % halves
-                    push((u + 1) // halves, gz, jnp.where(near_top, 1 - later, later))
+                pl.when((d == 1) & more)(lambda: push(next_f, gz, next_h))
+                pl.when((d == 2) & more)(lambda: pass_end(u + 1))
+                pl.when((d == 1) & (f > 0))(lambda: rest_half(f - 1, v))
+                first = jnp.where((d == 2) & more, 0, 1)
+
+                def one(i):
+                    own_turn = i == 0
+                    work(
+                        jnp.where(own_turn, next_f, f),
+                        jnp.where(own_turn, gz, slab),
+                        jnp.where(own_turn, next_h, h),
+                    )
+
+                each(2, one, first)
 
             each(nz - 1, at, 1)
             choose(f, h, beyond, stage, False)
             for part in range(2):
                 to_end(f, h, part).start()
 
+            @pl.when((v == halves - 1) & (f > 0))
+            def _():
+                each(halves, lambda i: choose(f - 1, i, total, out, False))
+
         each_half(phase)
-        rest(freqs - 1, end)
+        each(halves, lambda v: rest_half(freqs - 1, v))
         each(halves, lambda h: choose(freqs - 1, h, total, out, False))
 
     if nz > 4:

time: 161 us -> 151 us (0.938); the launches traced: 161 us -> 148 us
  Pallas kernels: 156 us -> 144 us
    pallas_call x1, Pallas kernels: 156 us -> 144 us  [per_device(): pl.pallas_call(functools.partial(kernel, nx, ny, nz), out_shape=jax.Shape...]
where the time goes in v5:
time: 151 us; the launch traced here: 148 us
  Pallas kernels  144 us (95%)
  local copies, waits for them, and re-layouts  4.91 us (3%)
    pallas_call x1, Pallas kernels, per_device(): pl.pallas_call(functools.partial(kernel, nx, ny, nz), out_shape=jax.Shape...  144 us
    unnamed x1, local copies, waits for them, and re-layouts  4.91 us

profile of v5, /device:TPU:4, one launch (start us, length us, event | category | flops | bytes accessed | tf_op | source)
XLA Modules:
  0.0 148.4 jit_solution(2354916139635496492)
XLA Ops:
  0.0 143.5 %shard_map.28 = f32[2,2,4,2,64,512]{5,4,3,2,1,0:T(8,128)} custom-call(bf16[2,2,2,2,256,256]{5,4,3,2,1,0:T(8,128)(2,1)} %green.1, s32[2,4]{1,0:T(2,128)} %bitcast.1), custom_call_target="tpu_custom_call" | custom-call | flops 5368709120 | bytes 12582912 | tf_op jit(solution)/shard_map/pallas_call | solution.py:424
  143.5 4.9 %copy.4 = f32[2,2,4,2,64,512]{5,4,3,2,1,0:T(8,128)} copy(f32[2,2,4,2,64,512]{5,4,3,2,1,0:T(8,128)} %shard_map.28) | data formatting | bytes 8388608

commit v6 on v5

--- a/solution.py
+++ b/solution.py
@@ -9,6 +9,7 @@
 
 MESH = pl.DeviceIdType.MESH
 CANDIDATES = ((0, 0), (0, 1), (1, -1), (1, 0), (1, 1))
+GROUPS = ((0, 3), (1, 4), (2,))
 
 
 def kernel(
@@ -162,38 +163,49 @@
                     left[base : base + width, traces:] = imag
                     left[base + width : base + 2 * width, :traces] = -imag
                     left[base + width : base + 2 * width, traces:] = real
-                for c, (dx, dy) in enumerate(CANDIDATES):
-                    ox, oy = tx + dx, ty + dy
-                    there = True
+                def tile(ox, oy):
                     if ox == tiles_x:
-                        there = has_right
-                        beside = right.at[f, slab, h, oy + 1]
-                    elif oy == tiles_y:
-                        beside = up.at[f, slab, h, ox]
-                    elif oy < 0:
-                        beside = down.at[f, slab, h, ox]
-                    else:
-                        beside = own.at[f, slab, h, ox, oy]
+                        return right.at[f, slab, h, oy + 1]
                     if oy == tiles_y:
-                        there = there & has_up
+                        return up.at[f, slab, h, ox]
                     if oy < 0:
-                        there = there & has_down
-
-                    def add(beside=beside, c=c):
-                        block = jnp.dot(
-                            left[:rows], beside[...].reshape(2 * traces, lanes),
-                            preferred_element_type=jnp.float32,
-                        )
+                        return down.at[f, slab, h, ox]
+                    return own.at[f, slab, h, ox, oy]
+
+                def add(group):
+                    beside = [
+                        tile(tx + CANDIDATES[c][0], ty + CANDIDATES[c][1])[...].reshape(2 * traces, lanes)
+                        for c in group
+                    ]
+                    blocks = jnp.dot(
+                        left[:rows], jnp.concatenate(beside, axis=1) if len(group) > 1 else beside[0],
+                        preferred_element_type=jnp.float32,
+                    )
+                    for i, c in enumerate(group):
+                        block = blocks[:, i * lanes : (i + 1) * lanes]
                         total[f, tx, ty, c, h, :, :lanes] += block[:width]
                         total[f, tx, ty, c, h, :, lanes:] += block[width : 2 * width]
                         if both:
                             beyond[f, tx, ty, c, h, :, :lanes] += block[2 * width : 3 * width]
                             beyond[f, tx, ty, c, h, :, lanes:] += block[3 * width :]
 
+                def run(group, there):
                     if there is True:
-                        add()
+                        add(group)
                     else:
-                        pl.when(there)(add)
+                        pl.when(there)(lambda: add(group))
+
+                for group in GROUPS:
+                    oy = ty + CANDIDATES[group[0]][1]
+                    there = has_up if oy == tiles_y else has_down if oy < 0 else True
+                    if tx + 1 < tiles_x:
+                        run(group, there)
+                        continue
+                    near_ones = tuple(c for c in group if CANDIDATES[c][0] == 0)
+                    run(group, has_right if there is True else there & has_right)
+                    if near_ones:
+                        alone = jnp.logical_not(has_right)
+                        run(near_ones, alone if there is True else there & alone)
 
     def choose(f, h, source, target, add):
         for k in range(pairs):
@@ -227,7 +239,7 @@
 
     @pl.when(at_end)
     def _():
-        each(phases, send_own, 1)
+        send_own(1)
         each_half(lambda f, v: push(f, gz, jnp.where(gz == 0, v, 1 - v)))
         total[...] = jnp.zeros_like(total)
 
@@ -236,6 +248,8 @@
             halo_y(f, gz, h)
             pl.when(has_up)(lambda: halo_up(f, h).start())
             pl.when(has_down)(lambda: halo_down(f, h).start())
+            u = f * halves + v
+            pl.when(u + 2 < phases)(lambda: send_own(u + 2))
 
         each_half(pass_halo)
 
@@ -281,10 +295,10 @@
             return jnp.where(near_top, 1 - v, v)
 
         def work(f, slab, h):
-            halo_y(f, slab, h)
             halo_x(f, slab, h)
             products(f, slab, h, True)
 
+        halo_y(0, gz, near_half(0))
         work(0, gz, near_half(0))
         pass_end(0)
 
@@ -319,6 +333,7 @@
 
                 def one(i):
                     own_turn = i == 0
+                    pl.when(i == 1)(lambda: halo_y(f, slab, h))
                     work(
                         jnp.where(own_turn, next_f, f),
                         jnp.where(own_turn, gz, slab),
@@ -326,6 +341,7 @@
                     )
 
                 each(2, one, first)
+                pl.when((d == 1) & more)(lambda: halo_y(next_f, gz, next_h))
 
             each(nz - 1, at, 1)
             choose(f, h, beyond, stage, False)

time: 151 us -> 148 us (0.980)
  Pallas kernels: 144 us -> 141 us
    pallas_call x1, Pallas kernels: 144 us -> 141 us  [per_device(): pl.pallas_call(functools.partial(kernel, nx, ny, nz), out_shape=jax.Shape...]
where the time goes in v6:
time: 148 us; the launch traced here: 145 us
  Pallas kernels  141 us (95%)
  local copies, waits for them, and re-layouts  4.91 us (3%)
    pallas_call x1, Pallas kernels, per_device(): pl.pallas_call(functools.partial(kernel, nx, ny, nz), out_shape=jax.Shape...  141 us
    unnamed x1, local copies, waits for them, and re-layouts  4.91 us

profile of v6, /device:TPU:4, one launch (start us, length us, event | category | flops | bytes accessed | tf_op | source)
XLA Modules:
  0.0 145.5 jit_solution(1350856661730998746)
XLA Ops:
  0.0 140.5 %shard_map.28 = f32[2,2,4,2,64,512]{5,4,3,2,1,0:T(8,128)} custom-call(bf16[2,2,2,2,256,256]{5,4,3,2,1,0:T(8,128)(2,1)} %green.1, s32[2,4]{1,0:T(2,128)} %bitcast.1), custom_call_target="tpu_custom_call" | custom-call | flops 5368709120 | bytes 12582912 | tf_op jit(solution)/shard_map/pallas_call | solution.py:440
  140.5 4.9 %copy.4 = f32[2,2,4,2,64,512]{5,4,3,2,1,0:T(8,128)} copy(f32[2,2,4,2,64,512]{5,4,3,2,1,0:T(8,128)} %shard_map.28) | data formatting | bytes 8388608

commit v7 on v6

--- a/solution.py
+++ b/solution.py
@@ -54,16 +54,16 @@
         here = own.at[f, slab, h]
         return remote(here, here, send_zd.at[f, slab, h], own_sem.at[f, slab, h], sa=gz - 1)
 
-    def y_down(f, slab, h):
+    def y_down(f, slab, h, tx):
         return remote(
-            own.at[f, slab, h, :, 0], up.at[f, slab, h],
-            send_yd.at[f, slab, h], up_sem.at[f, slab, h], gy=gy - 1,
-        )
-
-    def y_up(f, slab, h):
+            own.at[f, slab, h, tx, 0], up.at[f, slab, h, tx],
+            send_yd.at[f, slab, h, tx], up_sem.at[f, slab, h, tx], gy=gy - 1,
+        )
+
+    def y_up(f, slab, h, tx):
         return remote(
-            own.at[f, slab, h, :, tiles_y - 1], down.at[f, slab, h],
-            send_yu.at[f, slab, h], down_sem.at[f, slab, h], gy=gy + 1,
+            own.at[f, slab, h, tx, tiles_y - 1], down.at[f, slab, h, tx],
+            send_yu.at[f, slab, h, tx], down_sem.at[f, slab, h, tx], gy=gy + 1,
         )
 
     def x_left(kind, f, slab, h):
@@ -83,13 +83,13 @@
             send_end.at[f, h, part], end_sem.at[f, h, part], sa=beside_end,
         )
 
-    def halo_up(f, h):
-        here = up.at[f, gz, h]
-        return remote(here, here, send_halo.at[0, f, h], up_sem.at[f, gz, h], sa=inward)
-
-    def halo_down(f, h):
-        here = down.at[f, gz, h]
-        return remote(here, here, send_halo.at[1, f, h], down_sem.at[f, gz, h], sa=inward)
+    def halo_up(f, h, tx):
+        here = up.at[f, gz, h, tx]
+        return remote(here, here, send_halo.at[0, f, h, tx], up_sem.at[f, gz, h, tx], sa=inward)
+
+    def halo_down(f, h, tx):
+        here = down.at[f, gz, h, tx]
+        return remote(here, here, send_halo.at[1, f, h, tx], down_sem.at[f, gz, h, tx], sa=inward)
 
     def each(count, body, start=0):
         def step(i, carry):
@@ -119,20 +119,24 @@
         pl.when(has_left)(lambda: x_left(0, f, slab, h).start())
 
     def push(f, slab, h):
-        pl.when(has_down)(lambda: y_down(f, slab, h).start())
-        pl.when(has_up)(lambda: y_up(f, slab, h).start())
         push_x(f, slab, h)
+        for tx in range(tiles_x):
+            pl.when(has_down)(lambda: y_down(f, slab, h, tx).start())
+            pl.when(has_up)(lambda: y_up(f, slab, h, tx).start())
 
     def halo_y(f, slab, h):
-        @pl.when(has_up)
-        def _():
-            y_down(f, slab, h).wait_recv()
-            pl.when(has_left)(lambda: x_left(1, f, slab, h).start())
-
-        @pl.when(has_down)
-        def _():
-            y_up(f, slab, h).wait_recv()
-            pl.when(has_left)(lambda: x_left(2, f, slab, h).start())
+        for tx in range(tiles_x):
+            @pl.when(has_up)
+            def _():
+                y_down(f, slab, h, tx).wait_recv()
+                if tx == 0:
+                    pl.when(has_left)(lambda: x_left(1, f, slab, h).start())
+
+            @pl.when(has_down)
+            def _():
+                y_up(f, slab, h, tx).wait_recv()
+                if tx == 0:
+                    pl.when(has_left)(lambda: x_left(2, f, slab, h).start())
 
     def halo_x(f, slab, h):
         @pl.when(has_right)
@@ -246,8 +250,9 @@
         def pass_halo(f, v):
             h = jnp.where(gz == 0, v, 1 - v)
             halo_y(f, gz, h)
-            pl.when(has_up)(lambda: halo_up(f, h).start())
-            pl.when(has_down)(lambda: halo_down(f, h).start())
+            for tx in range(tiles_x):
+                pl.when(has_up)(lambda: halo_up(f, h, tx).start())
+                pl.when(has_down)(lambda: halo_down(f, h, tx).start())
             u = f * halves + v
             pl.when(u + 2 < phases)(lambda: send_own(u + 2))
 
@@ -278,13 +283,11 @@
             def _():
                 z_down(f, end, v).wait_recv()
                 z_down(f, end, v).start()
-                push_x(f, end, v)
 
             @pl.when(near_bottom)
             def _():
                 z_up(f, end, 1 - v).wait_recv()
                 z_up(f, end, 1 - v).start()
-                push_x(f, end, 1 - v)
 
             pl.when(u + 1 < phases)(lambda: send_own(u + 1))
 
@@ -301,6 +304,7 @@
         halo_y(0, gz, near_half(0))
         work(0, gz, near_half(0))
         pass_end(0)
+        push_x(0, end, jnp.where(near_top, 0, 1))
 
         def rest_half(f, v):
             h = jnp.where(near_top, v, 1 - v)
@@ -326,14 +330,21 @@
                     z_down(f, slab, h).wait_recv()
 
                 push(f, slab, h)
-                pl.when((d == 1) & more)(lambda: push(next_f, gz, next_h))
                 pl.when((d == 2) & more)(lambda: pass_end(u + 1))
                 pl.when((d == 1) & (f > 0))(lambda: rest_half(f - 1, v))
                 first = jnp.where((d == 2) & more, 0, 1)
 
                 def one(i):
                     own_turn = i == 0
-                    pl.when(i == 1)(lambda: halo_y(f, slab, h))
+
+                    @pl.when(i == 1)
+                    def _():
+                        halo_y(f, slab, h)
+                        pl.when((d == 1) & more)(lambda: push(next_f, gz, next_h))
+                        pl.when((d == 2) & more)(
+                            lambda: push_x(next_f, end, jnp.where(near_top, (u + 1) % halves, 1 - (u + 1) % halves))
+                        )
+
                     work(
                         jnp.where(own_turn, next_f, f),
                         jnp.where(own_turn, gz, slab),
@@ -398,13 +409,15 @@
 
             @pl.when(middle | (slab == gz) | (near & (slab != beside_end)))
             def _():
-                pl.when(has_down)(lambda: y_down(f, slab, h).wait_send())
-                pl.when(has_up)(lambda: y_up(f, slab, h).wait_send())
+                for tx in range(tiles_x):
+                    pl.when(has_down)(lambda: y_down(f, slab, h, tx).wait_send())
+                    pl.when(has_up)(lambda: y_up(f, slab, h, tx).wait_send())
 
             @pl.when(at_end & (slab == gz))
             def _():
-                pl.when(has_up)(lambda: halo_up(f, h).wait_send())
-                pl.when(has_down)(lambda: halo_down(f, h).wait_send())
+                for tx in range(tiles_x):
+                    pl.when(has_up)(lambda: halo_up(f, h, tx).wait_send())
+                    pl.when(has_down)(lambda: halo_down(f, h, tx).wait_send())
 
             @pl.when(inside | (slab == gz))
             def _():
@@ -454,17 +467,17 @@
             pltpu.VMEM((4 * width, 2 * traces), jnp.bfloat16),
             dma((freqs, halves)),
             dma(piece),
-            dma(piece),
-            dma(piece),
+            dma(piece + (tiles_x,)),
+            dma(piece + (tiles_x,)),
             dma((3,) + piece),
             dma((freqs, halves, 2)),
             dma(piece),
             dma(piece),
-            dma(piece),
-            dma(piece),
+            dma(piece + (tiles_x,)),
+            dma(piece + (tiles_x,)),
             dma((3,) + piece),
             dma((freqs, halves, 2)),
-            dma((2, freqs, halves)),
+            dma((2, freqs, halves, tiles_x)),
         ],
         compiler_params=pltpu.CompilerParams(
             collective_id=0, has_side_effects=True, vmem_limit_bytes=61 * 2**20

time: 148 us -> 149 us (level)
    pallas_call x1, Pallas kernels: 141 us -> 142 us  [per_device(): pl.pallas_call(functools.partial(kernel, nx, ny, nz), out_shape=jax.Shape...]
where the time goes in v7:
time: 149 us; the launch traced here: 147 us
  Pallas kernels  142 us (95%)
  local copies, waits for them, and re-layouts  4.91 us (3%)
    pallas_call x1, Pallas kernels, per_device(): pl.pallas_call(functools.partial(kernel, nx, ny, nz), out_shape=jax.Shape...  142 us
    unnamed x1, local copies, waits for them, and re-layouts  4.91 us

profile of v7, /device:TPU:4, one launch (start us, length us, event | category | flops | bytes accessed | tf_op | source)
XLA Modules:
  0.0 147.4 jit_solution(17458283652311351921)
XLA Ops:
  0.0 142.5 %shard_map.28 = f32[2,2,4,2,64,512]{5,4,3,2,1,0:T(8,128)} custom-call(bf16[2,2,2,2,256,256]{5,4,3,2,1,0:T(8,128)(2,1)} %green.1, s32[2,4]{1,0:T(2,128)} %bitcast.1), custom_call_target="tpu_custom_call" | custom-call | flops 5368709120 | bytes 12582912 | tf_op jit(solution)/shard_map/pallas_call | solution.py:453
  142.5 4.9 %copy.4 = f32[2,2,4,2,64,512]{5,4,3,2,1,0:T(8,128)} copy(f32[2,2,4,2,64,512]{5,4,3,2,1,0:T(8,128)} %shard_map.28) | data formatting | bytes 8388608

commit v8 on v6

--- a/solution.py
+++ b/solution.py
@@ -428,6 +428,10 @@
         each_half(body)
 
 
+def hand_on(source, target):
+    target[...] = source[...]
+
+
 def per_device(green, offsets):
     tiles_x, tiles_y, freqs, _, traces, points = green.shape
     nx, ny, nz = (lax.axis_size(name) for name in ("gx", "gy", "sa"))
@@ -437,7 +441,7 @@
     result = (tiles_x, tiles_y, pairs, freqs, width, 2 * points)
     sums = (freqs, tiles_x, tiles_y, len(CANDIDATES), halves, width, 2 * lanes)
     piece, cell = (freqs, nz, halves), (2, traces, lanes)
-    return pl.pallas_call(
+    blocks = pl.pallas_call(
         functools.partial(kernel, nx, ny, nz),
         out_shape=jax.ShapeDtypeStruct(result, jnp.float32),
         in_specs=[pl.BlockSpec(memory_space=pl.ANY), pl.BlockSpec(memory_space=pltpu.SMEM)],
@@ -474,6 +478,15 @@
             bytes_accessed=12 * 2**20, transcendentals=0,
         ),
     )(green, offsets.T)
+    rows = tiles_x * tiles_y * pairs * freqs * width
+    spec = pl.BlockSpec((rows // 8, 2 * points), lambda i: (i, 0))
+    return pl.pallas_call(
+        hand_on,
+        grid=(8,),
+        out_shape=jax.ShapeDtypeStruct((rows, 2 * points), jnp.float32),
+        in_specs=[spec],
+        out_specs=spec,
+    )(blocks.reshape(rows, 2 * points)).reshape(result)
 
 
 def solution(mesh):

time: 148 us -> 149 us (level)
  Pallas kernels: 141 us -> 147 us
  local copies, waits for them, and re-layouts: 4.91 us -> 0 us
    pallas_call x0 -> x1, Pallas kernels: none -> 6.59 us  [per_device(): pl.pallas_call(hand_on, grid=(8,), out_shape=jax.ShapeDtypeStruct((rows,...]
    unnamed x1 -> x0, local copies, waits for them, and re-layouts: 4.91 us -> none
where the time goes in v8:
time: 149 us; the launch traced here: 147 us
  Pallas kernels  147 us (99%)
    pallas_call x1, Pallas kernels, per_device(): pl.pallas_call(functools.partial(kernel, nx, ny, nz), out_shape=jax.Shape...  141 us
    pallas_call x1, Pallas kernels, per_device(): pl.pallas_call(hand_on, grid=(8,), out_shape=jax.ShapeDtypeStruct((rows,...  6.59 us

profile of v8, /device:TPU:4, one launch (start us, length us, event | category | flops | bytes accessed | tf_op | source)
XLA Modules:
  0.0 147.1 jit_solution(17497730785120306677)
XLA Ops:
  0.0 140.5 %shard_map.28 = f32[2,2,4,2,64,512]{5,4,3,2,1,0:T(8,128)} custom-call(bf16[2,2,2,2,256,256]{5,4,3,2,1,0:T(8,128)(2,1)} %green.1, s32[2,4]{1,0:T(2,128)} %bitcast.4), custom_call_target="tpu_custom_call" | custom-call | flops 5368709120 | bytes 12582912 | tf_op jit(solution)/shard_map/pallas_call | solution.py:444
  140.5 6.6 %shard_map.29 = f32[2048,512]{1,0:T(8,128)} custom-call(f32[2048,512]{1,0:T(8,128)} %bitcast.3), custom_call_target="tpu_custom_call" | custom-call | tf_op jit(solution)/shard_map/pallas_call | solution.py:483
